TPU v7x, 128 devices: a whole 4x4x4 slice. The times are simulated.
128 devices in a mesh: tm: 16 (over z_hi, y, core), space: 8 (over z_lo, x).
Axes of the slice: x: 4, y: 4, z: 4 (z_hi: 2, z_lo: 2; z = z_hi * 2 + z_lo), core: 2. Of those that a mesh axis runs over, the one named last changes fastest.
Arguments:
- forcing: float32 [16, 8, 512, 1024], P('tm', 'space'), may hold values from -6 to 6
- iterate: float32 [16, 8, 512, 1024], P('tm', 'space'), may hold values from -6 to 6
- forward_state: float32 [16, 8, 512, 1024], P('tm', 'space'), may hold values from -6 to 6
- conductivity: float32 [8, 512, 1024], P('space'), may hold values from 0.5 to 2
- terminal: float32 [8, 512, 1024], P('space'), may hold values from -6 to 6
Outputs:
- renewed: float32 [16, 8, 512, 1024], P('tm', 'space')
- gradient: float32 [8, 512, 1024], P('space', 'tm')
All inputs are finite; a program needn't handle non-finite values.
Results may differ from a plain program's by a relative error of at most 0.0003.
Values sent between devices are 32-bit elements; how exact they have to be, the bound alone decides.
A program may use at most 128 MiB of HBM per device.

v0:
```python
import functools
import math

import jax
import jax.numpy as jnp
import ml_dtypes
import numpy as np
from jax import lax
from jax.experimental import pallas as pl
from jax.experimental.pallas import tpu as pltpu
from jax.sharding import PartitionSpec as P

inv_dt = 4.0
wrap_alpha = 0.25
MESH = pl.DeviceIdType.MESH
stride = 37
parts = 4
f32, bf16 = jnp.float32, jnp.bfloat16


def table(length):
    j = np.arange(length)[:, None]
    c = np.arange(length)[None, :]
    angle = math.pi * ((j * (2 * c + 1)) % (4 * length)) / (2 * length)
    factor = np.where(j == 0, math.sqrt(1.0 / length), math.sqrt(2.0 / length))
    return factor * np.cos(angle)


def eigen(length):
    return 2.0 - 2.0 * np.cos(math.pi * np.arange(length) / length)


def halves(tab):
    hi = tab.astype(ml_dtypes.bfloat16)
    lo = (tab - hi.astype(np.float64)).astype(ml_dtypes.bfloat16)
    return np.stack([hi, lo])


def split(x):
    hi = x.astype(bf16)
    return hi, (x - hi.astype(f32)).astype(bf16)


def dot3(ah, al, bh, bl):
    d = lambda a, b: jnp.dot(a, b, preferred_element_type=f32)
    return d(ah, bh) + d(ah, bl) + d(al, bh)


def take(ref, sem):
    pltpu.make_async_copy(ref, ref, sem).wait()


def kernel(rows, cols, steps, layers,
           it_h, fo_h, fs_h, ka_h, te_h, qx_h, qxt_h, qy_h, qyt_h, ey_h, ex_h,
           rn_h, gr_h,
           itv, kav, fov, fsv, below, above, kbelow, kabove, prev,
           qx, qxt, qy, qyt, ey, ex,
           rh, rl, xh, xl, hat, spec, back, bh, bl, yh, yl, upd, fsc, rnc,
           face, edge, edges, tot, got, grad,
           local, halo_s, halo_r, prev_s, prev_r, k1s, k1r, k2s, k2r, k3s, k3r,
           fwd_s, fwd_r, bck_s, bck_r, fs_s, fs_r, rn_s, rn_r, ed_s, ed_r, gz_s, gz_r):
    tm, s = lax.axis_index("tm"), lax.axis_index("space")
    count = steps * layers
    me = tm * layers + s
    half, quarter = cols // 2, cols // 4
    part = rows // parts
    core, ypos, zhi = lax.rem(tm, 2), lax.rem(lax.div(tm, 2), 4), lax.div(tm, 8)

    def remote(src, dst, send, recv, to):
        return pltpu.make_async_remote_copy(src, dst, send, recv, device_id=to, device_id_type=MESH)

    def coords(d):
        return (lax.div(d, layers), lax.rem(d, layers))

    def sent(ref, sem):
        remote(ref, ref, sem, sem, (lax.rem(tm + 1, steps), s)).wait_send()

    body_it = itv.at[pl.ds(8, rows)]
    body_ka = kav.at[pl.ds(8, rows)]
    loads = [(it_h, body_it), (ka_h, body_ka), (fo_h, fov), (qxt_h, qxt), (qy_h, qy),
             (ey_h, ey), (ex_h, ex), (fs_h, fsv), (qx_h, qx), (qyt_h, qyt)]
    copies = [pltpu.make_async_copy(a, b, local.at[i]) for i, (a, b) in enumerate(loads)]
    for c in copies:
        c.start()

    barrier = pltpu.get_barrier_semaphore()

    def greet(i, c):
        pl.semaphore_signal(barrier, 1, device_id=coords(lax.rem(me + i, count)), device_id_type=MESH)
        return c

    lax.fori_loop(1, count, greet, 0)
    pl.semaphore_wait(barrier, count - 1)

    width = rows // 8

    def krows(y, c):
        return pl.ds(pl.multiple_of((y * 2 + c) * width, 8), width)

    mine = krows(ypos, core)
    not_last, not_first = s < layers - 1, s > 0
    k_up = remote(ka_h.at[mine], kbelow.at[mine], k1s.at[0], k1r.at[0], (tm, jnp.minimum(s + 1, layers - 1)))
    k_dn = remote(ka_h.at[mine], kabove.at[mine], k1s.at[1], k1r.at[1], (tm, jnp.maximum(s - 1, 0)))

    @pl.when(not_last)
    def _():
        k_up.start()

    @pl.when(not_first)
    def _():
        k_dn.start()

    @pl.when(s == 0)
    def _():
        pltpu.make_async_copy(ka_h.at[mine], kbelow.at[mine], k1r.at[0]).start()

    @pl.when(s == layers - 1)
    def _():
        pltpu.make_async_copy(ka_h.at[mine], kabove.at[mine], k1r.at[1]).start()

    def prows(i):
        return pl.ds(pl.multiple_of(i * part, 8), part)

    def halo_start(i, c):
        r = prows(i)

        @pl.when(not_last)
        def _():
            remote(it_h.at[r], below.at[r], halo_s.at[0, i], halo_r.at[0, i], (tm, jnp.minimum(s + 1, layers - 1))).start()

        @pl.when(not_first)
        def _():
            remote(it_h.at[r], above.at[r], halo_s.at[1, i], halo_r.at[1, i], (tm, jnp.maximum(s - 1, 0))).start()

        @pl.when(tm < steps - 1)
        def _():
            remote(it_h.at[r], prev.at[r], prev_s.at[i], prev_r.at[i], (jnp.minimum(tm + 1, steps - 1), s)).start()

        @pl.when(s == 0)
        def _():
            pltpu.make_async_copy(it_h.at[r], below.at[r], halo_r.at[0, i]).start()

        @pl.when(s == layers - 1)
        def _():
            pltpu.make_async_copy(it_h.at[r], above.at[r], halo_r.at[1, i]).start()

        @pl.when(tm == 0)
        def _():
            pltpu.make_async_copy(te_h.at[r], prev.at[r], prev_r.at[i]).start()

        return c

    lax.fori_loop(0, parts, halo_start, 0)

    for i in range(3):
        copies[i].wait()

    lane = lax.broadcasted_iota(jnp.int32, (8, cols), 1)
    sub = lax.broadcasted_iota(jnp.int32, (8, cols), 0)

    def in_plane(b, c):
        r = pl.multiple_of(b * 8, 8)
        vs, ks = itv[pl.ds(r, 24), :], kav[pl.ds(r, 24), :]
        v, vu, vd = vs[8:16], vs[9:17], vs[7:15]
        k, ku, kd = ks[8:16], ks[9:17], ks[7:15]
        fx = 0.5 * (pltpu.roll(k, cols - 1, 1) + k) * (pltpu.roll(v, cols - 1, 1) - v)
        fx = jnp.where(lane == cols - 1, 0.0, fx)
        fu = jnp.where(sub + r == rows - 1, 0.0, 0.5 * (ku + k) * (vu - v))
        fd = jnp.where(sub + r == 0, 0.0, 0.5 * (k + kd) * (v - vd))
        applied = (pltpu.roll(fx, 1, 1) - fx) + (fd - fu)
        fov[pl.ds(r, 8), :] = fov[pl.ds(r, 8), :] - (inv_dt * v + applied)
        return c

    blocks = rows // 8
    lax.fori_loop(0, blocks // 4, in_plane, 0)
    take(kbelow.at[mine], k1r.at[0])
    take(kabove.at[mine], k1r.at[1])

    def along_y(i, c):
        to = (zhi * 8 + lax.rem(ypos + i, 4) * 2 + core, s)
        remote(kbelow.at[mine], kbelow.at[mine], k2s, k2r, to).start()
        remote(kabove.at[mine], kabove.at[mine], k2s, k2r, to).start()
        return c

    lax.fori_loop(1, 4, along_y, 0)
    lax.fori_loop(blocks // 4, blocks, in_plane, 0)
    take(kbelow.at[pl.ds(0, 6 * width)], k2r)

    def across(i, c):
        r = krows(i, core)
        to = (zhi * 8 + ypos * 2 + 1 - core, s)
        remote(kbelow.at[r], kbelow.at[r], k3s, k3r, to).start()
        remote(kabove.at[r], kabove.at[r], k3s, k3r, to).start()
        return c

    lax.fori_loop(0, 4, across, 0)
    take(kbelow, k3r)
    copies[3].wait()

    def fs_send(i, c):
        d = lax.rem(me + i * stride, count)
        src = fs_h.at[pl.ds(pl.multiple_of(lax.div(d, 2) * 8, 8), 8), pl.ds(pl.multiple_of(lax.rem(d, 2) * half, half), half)]
        remote(src, fsc.at[me], fs_s, fs_r, coords(d)).start()
        return c

    def arrive(i, c):
        r = prows(i)
        take(below.at[r], halo_r.at[0, i])
        take(above.at[r], halo_r.at[1, i])
        take(prev.at[r], prev_r.at[i])

        def resid(b, c):
            q = pl.multiple_of(i * part + b * 16, 16)
            at = lambda ref, off=0: ref[pl.ds(q + off, 16), :]
            v, k = at(itv, 8), at(kav, 8)
            x = at(fov) + inv_dt * at(prev)
            x = x - 0.5 * (k + at(kbelow)) * (v - at(below)) - 0.5 * (k + at(kabove)) * (v - at(above))
            hi, lo = split(x)
            o = pl.multiple_of(b * 16, 16)
            rh[pl.ds(o, 16), :] = hi
            rl[pl.ds(o, 16), :] = lo
            return c

        lax.fori_loop(0, part // 16, resid, 0)
        for n in range(4):
            cs = slice(n * quarter, (n + 1) * quarter)
            acc = dot3(rh[...], rl[...], qxt[0, :, cs], qxt[1, :, cs])
            hi, lo = split(acc)
            xh[pl.ds(pl.multiple_of(i * part, 16), part), cs] = hi
            xl[pl.ds(pl.multiple_of(i * part, 16), part), cs] = lo
        return c

    lax.fori_loop(0, parts, arrive, 0)
    copies[4].wait()

    my_rows = pl.ds(pl.multiple_of(lax.div(me, 2) * 8, 8), 8)

    def piece(d, p):
        return (pl.ds(pl.multiple_of(lax.div(d, 2) * 8, 8), 8),
                pl.ds(pl.multiple_of(p * half + lax.rem(d, 2) * quarter, quarter), quarter))

    for p in range(2):
        for n in range(2):
            cs = slice(p * half + n * quarter, p * half + (n + 1) * quarter)
            hat[:, cs] = dot3(qy[0], qy[1], xh[:, cs], xl[:, cs])

        def fwd(i, c, p=p):
            d = lax.rem(me + i * stride, count)
            remote(hat.at[piece(d, p)], spec.at[p, me], fwd_s.at[p], fwd_r.at[p], coords(d)).start()
            return c

        lax.fori_loop(1, count, fwd, 0)
        spec[p, me] = hat[piece(me, p)]

    lax.fori_loop(1, count, fs_send, 0)
    own_fs = pltpu.make_async_copy(fs_h.at[my_rows, pl.ds(pl.multiple_of(lax.rem(me, 2) * half, half), half)], fsc.at[me], local.at[10])
    own_fs.start()

    copies[5].wait()
    copies[6].wait()
    tab = table(layers)
    lam = eigen(layers)
    lz = layers // 2
    for p in range(2):
        take(spec.at[p, pl.ds(0, count - 1)], fwd_r.at[p])
        mu = ey[my_rows, :] + ex[:, pl.ds(pl.multiple_of(p * half + lax.rem(me, 2) * quarter, quarter), quarter)]
        w = [1.0 / (mu + (inv_dt + float(lam[j]))) for j in range(layers)]
        q = [inv_dt * w[j] for j in range(layers)]

        def forward(m, state, p=p, w=w, q=q):
            v = [spec[p, m * layers + z] for z in range(layers)]
            even = [v[z] + v[layers - 1 - z] for z in range(lz)]
            odd = [v[z] - v[layers - 1 - z] for z in range(lz)]
            new = []
            for j in range(layers):
                src = odd if j % 2 else even
                acc = src[0] * float(tab[j, 0])
                for z in range(1, lz):
                    acc = acc + src[z] * float(tab[j, z])
                u = q[j] * state[j] + w[j] * acc
                spec[p, m * layers + j] = u
                new.append(u)
            return tuple(new)

        state = lax.fori_loop(0, steps, forward, tuple(jnp.zeros((8, quarter), f32) for _ in range(layers)))
        carry = []
        for j in range(layers):
            t = q[j]
            for _ in range(int(math.log2(steps))):
                t = t * t
            carry.append(wrap_alpha * state[j] / (1.0 - wrap_alpha * t))

        def backward(m, carry, p=p, q=q):
            carry = tuple(q[j] * carry[j] for j in range(layers))
            u = [spec[p, m * layers + j] + carry[j] for j in range(layers)]
            for z in range(lz):
                e = u[0] * float(tab[0, z])
                o = u[1] * float(tab[1, z])
                for j in range(2, layers, 2):
                    e = e + u[j] * float(tab[j, z])
                    o = o + u[j + 1] * float(tab[j + 1, z])
                spec[p, m * layers + z] = e + o
                spec[p, m * layers + layers - 1 - z] = e - o
            return carry

        lax.fori_loop(0, steps, backward, tuple(carry))

        def bck(i, c, p=p):
            d = lax.rem(me + i * stride, count)
            remote(spec.at[p, d], back.at[piece(me, p)], bck_s.at[p], bck_r.at[p], coords(d)).start()
            return c

        lax.fori_loop(1, count, bck, 0)
        back[piece(me, p)] = spec[p, me]

    copies[8].wait()
    copies[9].wait()

    def to_plane(p):
        take(spec.at[p, pl.ds(0, count - 1)], bck_r.at[p])
        for n in range(2):
            cs = slice(p * half + n * quarter, p * half + (n + 1) * quarter)
            hi, lo = split(back[:, cs])
            acc = dot3(qyt[0], qyt[1], hi, lo)
            hi, lo = split(acc)
            yh[:, n * quarter:(n + 1) * quarter] = hi
            yl[:, n * quarter:(n + 1) * quarter] = lo

    def along_x(p, r, n):
        cs = slice(n * quarter, (n + 1) * quarter)
        ks = slice(p * half, (p + 1) * half)
        return dot3(yh[r, :], yl[r, :], qx[0, ks, cs], qx[1, ks, cs])

    to_plane(0)

    def first(i, c):
        r = pl.ds(pl.multiple_of(i * part, 16), part)
        for n in range(4):
            cs = slice(n * quarter, (n + 1) * quarter)
            upd[r, cs] = itv[pl.ds(pl.multiple_of(i * part, 16) + 8, part), cs] + along_x(0, r, n)
        return c

    lax.fori_loop(0, parts, first, 0)
    to_plane(1)
    per = count // parts

    def second(i, c):
        g = lax.rem(i + me, parts)
        start = pl.multiple_of(g * part, 16)
        r = pl.ds(start, part)
        for n in range(4):
            cs = slice(n * quarter, (n + 1) * quarter)
            upd[r, cs] = upd[r, cs] + along_x(1, r, n)

        def rn_send(j, c):
            d = g * per + lax.rem(me + j * 5, per)
            src = upd.at[pl.ds(pl.multiple_of(lax.div(d, 2) * 8, 8), 8), pl.ds(pl.multiple_of(lax.rem(d, 2) * half, half), half)]

            @pl.when(d != me)
            def _():
                remote(src, rnc.at[me], rn_s, rn_r, coords(d)).start()

            return c

        lax.fori_loop(0, per, rn_send, 0)
        pltpu.make_async_copy(upd.at[r], rn_h.at[r], local.at[11]).start()
        return c

    lax.fori_loop(0, parts, second, 0)
    rnc[me] = upd[my_rows, pl.ds(pl.multiple_of(lax.rem(me, 2) * half, half), half)]

    copies[7].wait()
    nb = rows // 8
    face[0:1, :] = jnp.zeros((1, cols), f32)
    face[pl.ds(nb, 8), :] = jnp.zeros((8, cols), f32)
    for f in range(1, nb):
        d_rn = upd[8 * f:8 * f + 1, :] - upd[8 * f - 1:8 * f, :]
        d_fs = fsv[8 * f:8 * f + 1, :] - fsv[8 * f - 1:8 * f, :]
        face[f:f + 1, :] = 0.5 * d_rn * d_fs
    tall = rows // steps
    eye = lax.broadcasted_iota(jnp.int32, (tall, 128), 0) == lax.broadcasted_iota(jnp.int32, (tall, 128), 1)
    row8 = lax.broadcasted_iota(jnp.int32, (8, cols), 0)

    for g in range(steps):
        r = slice(g * tall, (g + 1) * tall)
        d_rn = upd[r, half:half + 128] - pltpu.roll(upd[r, half - 128:half], 1, 1)
        d_fs = fsv[r, half:half + 128] - pltpu.roll(fsv[r, half - 128:half], 1, 1)
        px = 0.5 * d_rn * d_fs
        line = jnp.sum(jnp.where(eye, px[:, 0:1], 0.0), axis=0, keepdims=True)
        edge[g] = face[g * (tall // 8):g * (tall // 8) + 8, :]
        edge[g, 5:6, 0:128] = line

    def edge_send(i, c):
        g = lax.rem(tm + i, steps)
        remote(edge.at[g], edges.at[tm], ed_s, ed_r, (g, s)).start()
        return c

    lax.fori_loop(1, steps, edge_send, 0)
    edges[tm] = edge[tm]

    take(fsc.at[pl.ds(0, count - 1)], fs_r)
    own_fs.wait()
    take(rnc.at[pl.ds(0, count - 1)], rn_r)
    lane8 = lax.broadcasted_iota(jnp.int32, (8, half), 1)
    sub8 = lax.broadcasted_iota(jnp.int32, (8, half), 0)
    zero = jnp.zeros((8, half), f32)
    fz = zero
    for z in range(layers):

        def gather(t, c, z=z):
            fx, fy, fzz = c
            a, b = rnc[t * layers + z], fsc[t * layers + z]
            fx = fx + (pltpu.roll(a, half - 1, 1) - a) * (pltpu.roll(b, half - 1, 1) - b)
            fy = fy + (pltpu.roll(a, 7, 0) - a) * (pltpu.roll(b, 7, 0) - b)
            if z < layers - 1:
                fzz = fzz + (rnc[t * layers + z + 1] - a) * (fsc[t * layers + z + 1] - b)
            return fx, fy, fzz

        fx, fy, nz = lax.fori_loop(0, steps, gather, (zero, zero, zero))
        fx = jnp.where(lane8 == half - 1, 0.0, fx)
        fy = jnp.where(sub8 == 7, 0.0, fy)
        tot[z] = 0.5 * (fx + pltpu.roll(fx, 1, 1) + fy + pltpu.roll(fy, 1, 0) + fz + nz)
        fz = nz

    def tot_send(i, c):
        z = lax.rem(s + i, layers)
        remote(tot.at[z], got.at[s], gz_s, gz_r, (tm, z)).start()
        return c

    lax.fori_loop(1, layers, tot_send, 0)
    got[s] = tot[s]
    take(edges.at[pl.ds(0, steps - 1)], ed_r)
    total = edges[0]
    for t in range(1, steps):
        total = total + edges[t]
    face[0:8, :] = total
    column = jnp.sum(jnp.where(eye, face[5:6, 0:128], 0.0), axis=1, keepdims=True)
    take(got.at[pl.ds(0, layers - 1)], gz_r)
    for r in range(tall // 8):
        for h in range(2):
            cs = slice(h * half, (h + 1) * half)
            val = got[2 * r + h]
            val = val + jnp.where(sub8 == 0, face[r:r + 1, cs], 0.0)
            val = val + jnp.where(sub8 == 7, face[r + 1:r + 2, cs], 0.0)
            val = val + jnp.where(lane8 == (half - 1 if h == 0 else 0), column[8 * r:8 * r + 8], 0.0)
            grad[8 * r:8 * r + 8, cs] = val * (-1.0 / steps)
    out = pltpu.make_async_copy(grad, gr_h, local.at[12])
    out.start()

    @pl.when(not_last)
    def _():
        sent(kbelow.at[mine], k1s.at[0])
        for i in range(parts):
            sent(below.at[prows(i)], halo_s.at[0, i])

    @pl.when(not_first)
    def _():
        sent(kabove.at[mine], k1s.at[1])
        for i in range(parts):
            sent(above.at[prows(i)], halo_s.at[1, i])

    @pl.when(tm < steps - 1)
    def _():
        for i in range(parts):
            sent(prev.at[prows(i)], prev_s.at[i])

    sent(kbelow.at[pl.ds(0, 6 * width)], k2s)
    sent(kbelow, k3s)
    for p in range(2):
        sent(spec.at[p, pl.ds(0, count - 1)], fwd_s.at[p])
        sent(spec.at[p, pl.ds(0, count - 1)], bck_s.at[p])
    sent(fsc.at[pl.ds(0, count - 1)], fs_s)
    sent(rnc.at[pl.ds(0, count - 1)], rn_s)
    sent(edges.at[pl.ds(0, steps - 1)], ed_s)
    sent(got.at[pl.ds(0, layers - 1)], gz_s)
    take(upd, local.at[11])
    out.wait()


def body(forcing, iterate, forward_state, conductivity, terminal):
    rows, cols = iterate.shape[2:]
    steps, layers = lax.axis_size("tm"), lax.axis_size("space")
    count, half, quarter, part = steps * layers, cols // 2, cols // 4, rows // parts
    tx, ty = halves(table(cols)), halves(table(rows))
    ey = np.broadcast_to(eigen(rows)[:, None], (rows, quarter)).astype(np.float32)
    ex = np.broadcast_to(eigen(cols)[None, :], (8, cols)).astype(np.float32)
    consts = [tx, tx.transpose(0, 2, 1), ty, ty.transpose(0, 2, 1), ey, ex]
    consts = [jnp.asarray(np.ascontiguousarray(c)) for c in consts]
    V = pltpu.VMEM
    D = pltpu.SemaphoreType.DMA
    plane = V((rows, cols), f32)
    padded = V((rows + 16, cols), f32)
    scratch = [
        padded, padded, plane, plane, plane, plane, plane, plane, plane,
        V((2, cols, cols), bf16), V((2, cols, cols), bf16), V((2, rows, rows), bf16), V((2, rows, rows), bf16),
        V((rows, quarter), f32), V((8, cols), f32),
        V((part, cols), bf16), V((part, cols), bf16), V((rows, cols), bf16), V((rows, cols), bf16),
        plane, V((2, count, 8, quarter), f32), plane,
        V((8, 128), bf16), V((8, 128), bf16), V((rows, half), bf16), V((rows, half), bf16),
        plane, V((count, 8, half), f32), V((count, 8, half), f32),
        V((rows // 8 + 8, cols), f32), V((steps, 8, cols), f32), V((steps, 8, cols), f32),
        V((layers, 8, half), f32), V((layers, 8, half), f32), V((rows // steps, cols), f32),
        D((13,)), D((2, parts)), D((2, parts)), D((parts,)), D((parts,)), D((2,)), D((2,)), D, D, D, D,
        D((2,)), D((2,)), D((2,)), D((2,)), D, D, D, D, D, D, D, D,
    ]

    anywhere = pl.BlockSpec(memory_space=pl.ANY)
    rn, gr = pl.pallas_call(
        functools.partial(kernel, rows, cols, steps, layers),
        in_specs=[anywhere] * 11,
        out_specs=[anywhere] * 2,
        out_shape=[jax.ShapeDtypeStruct((rows, cols), f32), jax.ShapeDtypeStruct((rows // steps, cols), f32)],
        scratch_shapes=scratch,
        compiler_params=pltpu.CompilerParams(collective_id=0, has_side_effects=True, vmem_limit_bytes=58 << 20),
        name="correction",
    )(iterate[0, 0], forcing[0, 0], forward_state[0, 0], conductivity[0], terminal[0], *consts)
    return rn[None, None], gr[None]


def solution(mesh):
    field, layer = P("tm", "space", None, None), P("space", None, None)
    return jax.shard_map(
        body,
        mesh=mesh,
        in_specs=(field, field, field, layer, layer),
        out_specs=(field, P("space", "tm", None)),
        check_vma=False,
    )
```

profile of v0, /device:TPU:1, one launch (start us, length us, event | category | flops | bytes accessed | tf_op | source)
XLA Modules:
  0.0 246.2 jit_solution(13334615003604615508)
XLA Ops:
  0.6 241.7 %correction.1 = (f32[512,1024]{1,0:T(8,128)}, f32[32,1024]{1,0:T(8,128)}) custom-call(f32[512,1024]{1,0:T(8,128)} %bitcast.8, f32[512,1024]{1,0:T(8,128)} %bitcast.9, f32[512,1024]{1,0:T(8,128)} %bitcast.10, f32[512,1024]{1,0:T(8,128)} %bitcast.11, f32[512,1024]{1,0:T(8,128)} %bitcast.12, bf16[2,1024,1024]{2,1,0:T(8,128)(2,1)} %constant.12.clone.qx_h, ...), custom_call_target="tpu_custom_call" | custom-call | tf_op jit(solution)/shard_map/correction/pallas_call | solution.py:508
  242.3 0.0 copy-start
  242.3 3.2 %copy.15 = f32[1,1,512,1024]{3,2,1,0:T(8,128)} copy(f32[1,1,512,1024]{3,2,1,0:T(8,128)} %bitcast.7) | data formatting | bytes 4194304
  245.5 0.0 copy-done
  245.5 0.7 copy.16
Async XLA Ops:
  242.3 3.2 %copy-start = (f32[32,1024]{1,0:T(8,128)S(1)}, f32[32,1024]{1,0:T(8,128)}, u32[]{:S(2)}) copy-start(f32[32,1024]{1,0:T(8,128)} %get-tuple-element.5) | copy-start | bytes 393220
where the time goes:
time: 247 us; the launch traced here: 246 us
  Pallas kernels  242 us (98%)
  local copies, waits for them, and re-layouts  3.85 us (2%)
    pallas_call x1, Pallas kernels, body(): pl.pallas_call(functools.partial(kernel, rows, cols, steps, layers), in_s...  242 us

commit v1 on v0

--- a/solution.py
+++ b/solution.py
@@ -15,6 +15,7 @@
 MESH = pl.DeviceIdType.MESH
 stride = 37
 parts = 4
+FS1, FS2 = 40, 128
 f32, bf16 = jnp.float32, jnp.bfloat16
 
 
@@ -53,11 +54,11 @@
 def kernel(rows, cols, steps, layers,
            it_h, fo_h, fs_h, ka_h, te_h, qx_h, qxt_h, qy_h, qyt_h, ey_h, ex_h,
            rn_h, gr_h,
-           itv, kav, fov, fsv, below, above, kbelow, kabove, prev,
+           itv, kav, fov, fsv, below, above, kbelow, kabove,
            qx, qxt, qy, qyt, ey, ex,
            rh, rl, xh, xl, hat, spec, back, bh, bl, yh, yl, upd, fsc, rnc,
-           face, edge, edges, tot, got, grad,
-           local, halo_s, halo_r, prev_s, prev_r, k1s, k1r, k2s, k2r, k3s, k3r,
+           face, edge, edges, tot, got, grad, dx, dxm, dy, dym, dz, acc5,
+           local, halo_s, halo_r, k1s, k1r, k2s, k2r, k3s, k3r,
            fwd_s, fwd_r, bck_s, bck_r, fs_s, fs_r, rn_s, rn_r, ed_s, ed_r, gz_s, gz_r):
     tm, s = lax.axis_index("tm"), lax.axis_index("space")
     count = steps * layers
@@ -132,10 +133,6 @@
         def _():
             remote(it_h.at[r], above.at[r], halo_s.at[1, i], halo_r.at[1, i], (tm, jnp.maximum(s - 1, 0))).start()
 
-        @pl.when(tm < steps - 1)
-        def _():
-            remote(it_h.at[r], prev.at[r], prev_s.at[i], prev_r.at[i], (jnp.minimum(tm + 1, steps - 1), s)).start()
-
         @pl.when(s == 0)
         def _():
             pltpu.make_async_copy(it_h.at[r], below.at[r], halo_r.at[0, i]).start()
@@ -144,16 +141,28 @@
         def _():
             pltpu.make_async_copy(it_h.at[r], above.at[r], halo_r.at[1, i]).start()
 
-        @pl.when(tm == 0)
-        def _():
-            pltpu.make_async_copy(te_h.at[r], prev.at[r], prev_r.at[i]).start()
-
         return c
 
     lax.fori_loop(0, parts, halo_start, 0)
 
     for i in range(3):
         copies[i].wait()
+    last = jnp.where(tm == steps - 1, 1.0, 0.0).astype(f32)
+    unit = 1.0 - last
+    four = inv_dt * last
+
+    @pl.when(tm == 0)
+    def _():
+        term = pltpu.make_async_copy(te_h, upd, local.at[13])
+        term.start()
+        term.wait()
+
+        def opening(b, c):
+            r = pl.ds(pl.multiple_of(b * 8, 8), 8)
+            fov[r, :] = fov[r, :] + inv_dt * upd[r, :]
+            return c
+
+        lax.fori_loop(0, rows // 8, opening, 0)
 
     lane = lax.broadcasted_iota(jnp.int32, (8, cols), 1)
     sub = lax.broadcasted_iota(jnp.int32, (8, cols), 0)
@@ -163,12 +172,12 @@
         vs, ks = itv[pl.ds(r, 24), :], kav[pl.ds(r, 24), :]
         v, vu, vd = vs[8:16], vs[9:17], vs[7:15]
         k, ku, kd = ks[8:16], ks[9:17], ks[7:15]
-        fx = 0.5 * (pltpu.roll(k, cols - 1, 1) + k) * (pltpu.roll(v, cols - 1, 1) - v)
+        fx = (0.5 * (pltpu.roll(k, cols - 1, 1) + k) - unit) * (pltpu.roll(v, cols - 1, 1) - v)
         fx = jnp.where(lane == cols - 1, 0.0, fx)
-        fu = jnp.where(sub + r == rows - 1, 0.0, 0.5 * (ku + k) * (vu - v))
-        fd = jnp.where(sub + r == 0, 0.0, 0.5 * (k + kd) * (v - vd))
+        fu = jnp.where(sub + r == rows - 1, 0.0, (0.5 * (ku + k) - unit) * (vu - v))
+        fd = jnp.where(sub + r == 0, 0.0, (0.5 * (k + kd) - unit) * (v - vd))
         applied = (pltpu.roll(fx, 1, 1) - fx) + (fd - fu)
-        fov[pl.ds(r, 8), :] = fov[pl.ds(r, 8), :] - (inv_dt * v + applied)
+        fov[pl.ds(r, 8), :] = fov[pl.ds(r, 8), :] - (four * v + applied)
         return c
 
     blocks = rows // 8
@@ -207,14 +216,13 @@
         r = prows(i)
         take(below.at[r], halo_r.at[0, i])
         take(above.at[r], halo_r.at[1, i])
-        take(prev.at[r], prev_r.at[i])
 
         def resid(b, c):
             q = pl.multiple_of(i * part + b * 16, 16)
             at = lambda ref, off=0: ref[pl.ds(q + off, 16), :]
             v, k = at(itv, 8), at(kav, 8)
-            x = at(fov) + inv_dt * at(prev)
-            x = x - 0.5 * (k + at(kbelow)) * (v - at(below)) - 0.5 * (k + at(kabove)) * (v - at(above))
+            x = at(fov) - (0.5 * (k + at(kbelow)) - unit) * (v - at(below))
+            x = x - (0.5 * (k + at(kabove)) - unit) * (v - at(above))
             hi, lo = split(x)
             o = pl.multiple_of(b * 16, 16)
             rh[pl.ds(o, 16), :] = hi
@@ -230,6 +238,7 @@
             xl[pl.ds(pl.multiple_of(i * part, 16), part), cs] = lo
         return c
 
+    lax.fori_loop(1, FS1, fs_send, 0)
     lax.fori_loop(0, parts, arrive, 0)
     copies[4].wait()
 
@@ -252,7 +261,7 @@
         lax.fori_loop(1, count, fwd, 0)
         spec[p, me] = hat[piece(me, p)]
 
-    lax.fori_loop(1, count, fs_send, 0)
+    lax.fori_loop(FS1, FS2, fs_send, 0)
     own_fs = pltpu.make_async_copy(fs_h.at[my_rows, pl.ds(pl.multiple_of(lax.rem(me, 2) * half, half), half)], fsc.at[me], local.at[10])
     own_fs.start()
 
@@ -313,6 +322,7 @@
         lax.fori_loop(1, count, bck, 0)
         back[piece(me, p)] = spec[p, me]
 
+    lax.fori_loop(FS2, count, fs_send, 0)
     copies[8].wait()
     copies[9].wait()
 
@@ -337,7 +347,7 @@
         r = pl.ds(pl.multiple_of(i * part, 16), part)
         for n in range(4):
             cs = slice(n * quarter, (n + 1) * quarter)
-            upd[r, cs] = itv[pl.ds(pl.multiple_of(i * part, 16) + 8, part), cs] + along_x(0, r, n)
+            upd[r, cs] = last * itv[pl.ds(pl.multiple_of(i * part, 16) + 8, part), cs] + along_x(0, r, n)
         return c
 
     lax.fori_loop(0, parts, first, 0)
@@ -345,7 +355,7 @@
     per = count // parts
 
     def second(i, c):
-        g = lax.rem(i + me, parts)
+        g = lax.rem(i + tm, parts)
         start = pl.multiple_of(g * part, 16)
         r = pl.ds(start, part)
         for n in range(4):
@@ -358,7 +368,7 @@
 
             @pl.when(d != me)
             def _():
-                remote(src, rnc.at[me], rn_s, rn_r, coords(d)).start()
+                remote(src, rnc.at[me], rn_s, rn_r.at[i], coords(d)).start()
 
             return c
 
@@ -400,26 +410,57 @@
 
     take(fsc.at[pl.ds(0, count - 1)], fs_r)
     own_fs.wait()
-    take(rnc.at[pl.ds(0, count - 1)], rn_r)
     lane8 = lax.broadcasted_iota(jnp.int32, (8, half), 1)
     sub8 = lax.broadcasted_iota(jnp.int32, (8, half), 0)
-    zero = jnp.zeros((8, half), f32)
-    fz = zero
+
+    def differences(j, c):
+        b = fsc[j]
+        x = jnp.where(lane8 == half - 1, 0.0, pltpu.roll(b, half - 1, 1) - b)
+        dx[j] = x
+        dxm[j] = pltpu.roll(x, 1, 1)
+        y = jnp.where(sub8 == 7, 0.0, pltpu.roll(b, 7, 0) - b)
+        dy[j] = y
+        dym[j] = pltpu.roll(y, 1, 0)
+        dz[j] = jnp.where(lax.rem(j, layers) == layers - 1, 0.0, fsc[jnp.minimum(j + 1, count - 1)] - b)
+        return c
+
+    lax.fori_loop(0, count, differences, 0, unroll=2)
+    zone = lax.div(tm, steps // parts)
+    acc5[...] = jnp.zeros_like(acc5)
+
+    def group(i, c):
+        low = lax.rem(zone - i + parts, parts)
+
+        @pl.when(low == lax.rem(tm, parts))
+        def _():
+            take(rnc.at[pl.ds(0, per - 1)], rn_r.at[i])
+
+        @pl.when(low != lax.rem(tm, parts))
+        def _():
+            take(rnc.at[pl.ds(0, per)], rn_r.at[i])
+
+        def layer(z, c):
+            sums = [acc5[z, f] for f in range(5)]
+            for k in range(steps // parts):
+                j = (low + parts * k) * layers + z
+                a = rnc[j]
+                up = rnc[jnp.where(z < layers - 1, j + 1, j)]
+                terms = (a * dx[j], a * dxm[j], a * dy[j], a * dym[j], (up - a) * dz[j])
+                sums = [p + q for p, q in zip(sums, terms)]
+            for f in range(5):
+                acc5[z, f] = sums[f]
+            return c
+
+        lax.fori_loop(0, layers, layer, 0)
+        return c
+
+    lax.fori_loop(0, parts, group, 0)
+    fz = jnp.zeros((8, half), f32)
     for z in range(layers):
-
-        def gather(t, c, z=z):
-            fx, fy, fzz = c
-            a, b = rnc[t * layers + z], fsc[t * layers + z]
-            fx = fx + (pltpu.roll(a, half - 1, 1) - a) * (pltpu.roll(b, half - 1, 1) - b)
-            fy = fy + (pltpu.roll(a, 7, 0) - a) * (pltpu.roll(b, 7, 0) - b)
-            if z < layers - 1:
-                fzz = fzz + (rnc[t * layers + z + 1] - a) * (fsc[t * layers + z + 1] - b)
-            return fx, fy, fzz
-
-        fx, fy, nz = lax.fori_loop(0, steps, gather, (zero, zero, zero))
-        fx = jnp.where(lane8 == half - 1, 0.0, fx)
-        fy = jnp.where(sub8 == 7, 0.0, fy)
-        tot[z] = 0.5 * (fx + pltpu.roll(fx, 1, 1) + fy + pltpu.roll(fy, 1, 0) + fz + nz)
+        sx, sxm, sy, sym, nz = [acc5[z, f] for f in range(5)]
+        fx = (sxm - sx) + pltpu.roll(sxm, half - 1, 1) - pltpu.roll(sx, 1, 1)
+        fy = (sym - sy) + pltpu.roll(sym, 7, 0) - pltpu.roll(sy, 1, 0)
+        tot[z] = 0.5 * (fx + fy + fz + nz)
         fz = nz
 
     def tot_send(i, c):
@@ -459,11 +500,6 @@
         for i in range(parts):
             sent(above.at[prows(i)], halo_s.at[1, i])
 
-    @pl.when(tm < steps - 1)
-    def _():
-        for i in range(parts):
-            sent(prev.at[prows(i)], prev_s.at[i])
-
     sent(kbelow.at[pl.ds(0, 6 * width)], k2s)
     sent(kbelow, k3s)
     for p in range(2):
@@ -491,7 +527,7 @@
     plane = V((rows, cols), f32)
     padded = V((rows + 16, cols), f32)
     scratch = [
-        padded, padded, plane, plane, plane, plane, plane, plane, plane,
+        padded, padded, plane, plane, plane, plane, plane, plane,
         V((2, cols, cols), bf16), V((2, cols, cols), bf16), V((2, rows, rows), bf16), V((2, rows, rows), bf16),
         V((rows, quarter), f32), V((8, cols), f32),
         V((part, cols), bf16), V((part, cols), bf16), V((rows, cols), bf16), V((rows, cols), bf16),
@@ -500,8 +536,9 @@
         plane, V((count, 8, half), f32), V((count, 8, half), f32),
         V((rows // 8 + 8, cols), f32), V((steps, 8, cols), f32), V((steps, 8, cols), f32),
         V((layers, 8, half), f32), V((layers, 8, half), f32), V((rows // steps, cols), f32),
-        D((13,)), D((2, parts)), D((2, parts)), D((parts,)), D((parts,)), D((2,)), D((2,)), D, D, D, D,
-        D((2,)), D((2,)), D((2,)), D((2,)), D, D, D, D, D, D, D, D,
+        *[V((count, 8, half), f32)] * 5, V((layers, 5, 8, half), f32),
+        D((14,)), D((2, parts)), D((2, parts)), D((2,)), D((2,)), D, D, D, D,
+        D((2,)), D((2,)), D((2,)), D((2,)), D, D, D, D((parts,)), D, D, D, D,
     ]
 
     anywhere = pl.BlockSpec(memory_space=pl.ANY)
@@ -511,7 +548,7 @@
         out_specs=[anywhere] * 2,
         out_shape=[jax.ShapeDtypeStruct((rows, cols), f32), jax.ShapeDtypeStruct((rows // steps, cols), f32)],
         scratch_shapes=scratch,
-        compiler_params=pltpu.CompilerParams(collective_id=0, has_side_effects=True, vmem_limit_bytes=58 << 20),
+        compiler_params=pltpu.CompilerParams(collective_id=0, has_side_effects=True, vmem_limit_bytes=60 << 20),
         name="correction",
     )(iterate[0, 0], forcing[0, 0], forward_state[0, 0], conductivity[0], terminal[0], *consts)
     return rn[None, None], gr[None]

time: 247 us -> 177 us (0.72)
  Pallas kernels: 242 us -> 170 us
    pallas_call x1, Pallas kernels: 242 us -> 170 us  [body(): pl.pallas_call(functools.partial(kernel, rows, cols, steps, layers), in_s...]
where the time goes in v1:
time: 177 us; the launch traced here: 174 us
  Pallas kernels  170 us (96%)
  local copies, waits for them, and re-layouts  3.85 us (2%)
    pallas_call x1, Pallas kernels, body(): pl.pallas_call(functools.partial(kernel, rows, cols, steps, layers), in_s...  170 us
    unnamed x4, local copies, waits for them, and re-layouts  3.85 us

profile of v1, /device:TPU:1, one launch (start us, length us, event | category | flops | bytes accessed | tf_op | source)
XLA Modules:
  0.0 174.3 jit_solution(7046430305707427805)
XLA Ops:
  0.6 169.8 %correction.1 = (f32[512,1024]{1,0:T(8,128)}, f32[32,1024]{1,0:T(8,128)}) custom-call(f32[512,1024]{1,0:T(8,128)} %bitcast.8, f32[512,1024]{1,0:T(8,128)} %bitcast.9, f32[512,1024]{1,0:T(8,128)} %bitcast.10, f32[512,1024]{1,0:T(8,128)} %bitcast.11, f32[512,1024]{1,0:T(8,128)} %bitcast.12, bf16[2,1024,1024]{2,1,0:T(8,128)(2,1)} %constant.12.clone.qx_h, ...), custom_call_target="tpu_custom_call" | custom-call | tf_op jit(solution)/shard_map/correction/pallas_call | solution.py:545
  170.4 0.0 copy-start
  170.5 3.2 %copy.15 = f32[1,1,512,1024]{3,2,1,0:T(8,128)} copy(f32[1,1,512,1024]{3,2,1,0:T(8,128)} %bitcast.7) | data formatting | bytes 4194304
  173.6 0.0 copy-done
  173.6 0.7 copy.16
Async XLA Ops:
  170.4 3.2 %copy-start = (f32[32,1024]{1,0:T(8,128)S(1)}, f32[32,1024]{1,0:T(8,128)}, u32[]{:S(2)}) copy-start(f32[32,1024]{1,0:T(8,128)} %get-tuple-element.5) | copy-start | bytes 393220

commit v2 on v1

--- a/solution.py
+++ b/solution.py
@@ -15,7 +15,7 @@
 MESH = pl.DeviceIdType.MESH
 stride = 37
 parts = 4
-FS1, FS2 = 40, 128
+FS1, FS2 = 32,96
 f32, bf16 = jnp.float32, jnp.bfloat16
 
 
@@ -86,11 +86,17 @@
 
     barrier = pltpu.get_barrier_semaphore()
 
-    def greet(i, c):
-        pl.semaphore_signal(barrier, 1, device_id=coords(lax.rem(me + i, count)), device_id_type=MESH)
-        return c
-
-    lax.fori_loop(1, count, greet, 0)
+    others = [lax.rem(s + b, layers) for b in range(layers)]
+    for b in range(1, layers):
+        pl.semaphore_signal(barrier, 1, device_id=(tm, others[b]), device_id_type=MESH)
+
+    def greet(a, c):
+        to = lax.rem(tm + a, steps)
+        for b in range(layers):
+            pl.semaphore_signal(barrier, 1, device_id=(to, others[b]), device_id_type=MESH)
+        return c
+
+    lax.fori_loop(1, steps, greet, 0)
     pl.semaphore_wait(barrier, count - 1)
 
     width = rows // 8

time: 177 us -> 174 us (0.983); the launches traced: 174 us -> 174 us
  no operation moved by 1% of the time
where the time goes in v2:
time: 174 us
  Pallas kernels  169 us (97%)
  local copies, waits for them, and re-layouts  3.85 us (2%)
    pallas_call x1, Pallas kernels, body(): pl.pallas_call(functools.partial(kernel, rows, cols, steps, layers), in_s...  169 us
    unnamed x4, local copies, waits for them, and re-layouts  3.85 us

profile of v2, /device:TPU:1, one launch (start us, length us, event | category | flops | bytes accessed | tf_op | source)
XLA Modules:
  0.0 173.5 jit_solution(16630106109336487790)
XLA Ops:
  0.6 169.0 %correction.1 = (f32[512,1024]{1,0:T(8,128)}, f32[32,1024]{1,0:T(8,128)}) custom-call(f32[512,1024]{1,0:T(8,128)} %bitcast.8, f32[512,1024]{1,0:T(8,128)} %bitcast.9, f32[512,1024]{1,0:T(8,128)} %bitcast.10, f32[512,1024]{1,0:T(8,128)} %bitcast.11, f32[512,1024]{1,0:T(8,128)} %bitcast.12, bf16[2,1024,1024]{2,1,0:T(8,128)(2,1)} %constant.12.clone.qx_h, ...), custom_call_target="tpu_custom_call" | custom-call | tf_op jit(solution)/shard_map/correction/pallas_call | solution.py:551
  169.7 0.0 copy-start
  169.7 3.2 %copy.15 = f32[1,1,512,1024]{3,2,1,0:T(8,128)} copy(f32[1,1,512,1024]{3,2,1,0:T(8,128)} %bitcast.7) | data formatting | bytes 4194304
  172.9 0.0 copy-done
  172.9 0.7 copy.16
Async XLA Ops:
  169.7 3.2 %copy-start = (f32[32,1024]{1,0:T(8,128)S(1)}, f32[32,1024]{1,0:T(8,128)}, u32[]{:S(2)}) copy-start(f32[32,1024]{1,0:T(8,128)} %get-tuple-element.5) | copy-start | bytes 393220

commit v3 on v2

--- a/solution.py
+++ b/solution.py
@@ -52,12 +52,12 @@
 
 
 def kernel(rows, cols, steps, layers,
-           it_h, fo_h, fs_h, ka_h, te_h, qx_h, qxt_h, qy_h, qyt_h, ey_h, ex_h,
+           it_h, fo_h, fs_h, ka_h, te_h, tab_h, eig_h,
            rn_h, gr_h,
            itv, kav, fov, fsv, below, above, kbelow, kabove,
            qx, qxt, qy, qyt, ey, ex,
            rh, rl, xh, xl, hat, spec, back, bh, bl, yh, yl, upd, fsc, rnc,
-           face, edge, edges, tot, got, grad, dx, dxm, dy, dym, dz, acc5,
+           face, edge, edges, tot, got, grad, acc5,
            local, halo_s, halo_r, k1s, k1r, k2s, k2r, k3s, k3r,
            fwd_s, fwd_r, bck_s, bck_r, fs_s, fs_r, rn_s, rn_r, ed_s, ed_r, gz_s, gz_r):
     tm, s = lax.axis_index("tm"), lax.axis_index("space")
@@ -76,6 +76,10 @@
     def sent(ref, sem):
         remote(ref, ref, sem, sem, (lax.rem(tm + 1, steps), s)).wait_send()
 
+    qx_h, qxt_h = tab_h.at[0:2], tab_h.at[2:4]
+    qy_h = tab_h.at[4:6, 0:rows, 0:rows]
+    qyt_h = tab_h.at[4:6, 0:rows, rows:2 * rows]
+    ey_h, ex_h = eig_h.at[0:rows, 0:quarter], eig_h.at[rows:rows + 8]
     body_it = itv.at[pl.ds(8, rows)]
     body_ka = kav.at[pl.ds(8, rows)]
     loads = [(it_h, body_it), (ka_h, body_ka), (fo_h, fov), (qxt_h, qxt), (qy_h, qy),
@@ -419,15 +423,25 @@
     lane8 = lax.broadcasted_iota(jnp.int32, (8, half), 1)
     sub8 = lax.broadcasted_iota(jnp.int32, (8, half), 0)
 
+    sent(kbelow.at[pl.ds(0, 6 * width)], k2s)
+    sent(kbelow, k3s)
+
+    def cell(j):
+        return (pl.ds(pl.multiple_of(lax.div(j, 2) * 8, 8), 8),
+                pl.ds(pl.multiple_of(lax.rem(j, 2) * half, half), half))
+
+    dx, dxm, dy, dym, dz = below, above, kbelow, kabove, fov
+
     def differences(j, c):
+        w = cell(j)
         b = fsc[j]
         x = jnp.where(lane8 == half - 1, 0.0, pltpu.roll(b, half - 1, 1) - b)
-        dx[j] = x
-        dxm[j] = pltpu.roll(x, 1, 1)
+        dx[w] = x
+        dxm[w] = pltpu.roll(x, 1, 1)
         y = jnp.where(sub8 == 7, 0.0, pltpu.roll(b, 7, 0) - b)
-        dy[j] = y
-        dym[j] = pltpu.roll(y, 1, 0)
-        dz[j] = jnp.where(lax.rem(j, layers) == layers - 1, 0.0, fsc[jnp.minimum(j + 1, count - 1)] - b)
+        dy[w] = y
+        dym[w] = pltpu.roll(y, 1, 0)
+        dz[w] = jnp.where(lax.rem(j, layers) == layers - 1, 0.0, fsc[jnp.minimum(j + 1, count - 1)] - b)
         return c
 
     lax.fori_loop(0, count, differences, 0, unroll=2)
@@ -449,9 +463,9 @@
             sums = [acc5[z, f] for f in range(5)]
             for k in range(steps // parts):
                 j = (low + parts * k) * layers + z
-                a = rnc[j]
+                a, w = rnc[j], cell(j)
                 up = rnc[jnp.where(z < layers - 1, j + 1, j)]
-                terms = (a * dx[j], a * dxm[j], a * dy[j], a * dym[j], (up - a) * dz[j])
+                terms = (a * dx[w], a * dxm[w], a * dy[w], a * dym[w], (up - a) * dz[w])
                 sums = [p + q for p, q in zip(sums, terms)]
             for f in range(5):
                 acc5[z, f] = sums[f]
@@ -506,8 +520,6 @@
         for i in range(parts):
             sent(above.at[prows(i)], halo_s.at[1, i])
 
-    sent(kbelow.at[pl.ds(0, 6 * width)], k2s)
-    sent(kbelow, k3s)
     for p in range(2):
         sent(spec.at[p, pl.ds(0, count - 1)], fwd_s.at[p])
         sent(spec.at[p, pl.ds(0, count - 1)], bck_s.at[p])
@@ -526,8 +538,12 @@
     tx, ty = halves(table(cols)), halves(table(rows))
     ey = np.broadcast_to(eigen(rows)[:, None], (rows, quarter)).astype(np.float32)
     ex = np.broadcast_to(eigen(cols)[None, :], (8, cols)).astype(np.float32)
-    consts = [tx, tx.transpose(0, 2, 1), ty, ty.transpose(0, 2, 1), ey, ex]
-    consts = [jnp.asarray(np.ascontiguousarray(c)) for c in consts]
+    tabs = np.zeros((6, cols, cols), ml_dtypes.bfloat16)
+    tabs[0:2], tabs[2:4] = tx, tx.transpose(0, 2, 1)
+    tabs[4:6, :rows, :rows], tabs[4:6, :rows, rows:2 * rows] = ty, ty.transpose(0, 2, 1)
+    eigs = np.zeros((2 * cols, cols), np.float32)
+    eigs[:rows, :quarter], eigs[rows:rows + 8] = ey, ex
+    consts = [jnp.asarray(tabs), jnp.asarray(eigs)]
     V = pltpu.VMEM
     D = pltpu.SemaphoreType.DMA
     plane = V((rows, cols), f32)
@@ -542,7 +558,7 @@
         plane, V((count, 8, half), f32), V((count, 8, half), f32),
         V((rows // 8 + 8, cols), f32), V((steps, 8, cols), f32), V((steps, 8, cols), f32),
         V((layers, 8, half), f32), V((layers, 8, half), f32), V((rows // steps, cols), f32),
-        *[V((count, 8, half), f32)] * 5, V((layers, 5, 8, half), f32),
+        V((layers, 5, 8, half), f32),
         D((14,)), D((2, parts)), D((2, parts)), D((2,)), D((2,)), D, D, D, D,
         D((2,)), D((2,)), D((2,)), D((2,)), D, D, D, D((parts,)), D, D, D, D,
     ]
@@ -550,11 +566,11 @@
     anywhere = pl.BlockSpec(memory_space=pl.ANY)
     rn, gr = pl.pallas_call(
         functools.partial(kernel, rows, cols, steps, layers),
-        in_specs=[anywhere] * 11,
+        in_specs=[anywhere] * 7,
         out_specs=[anywhere] * 2,
         out_shape=[jax.ShapeDtypeStruct((rows, cols), f32), jax.ShapeDtypeStruct((rows // steps, cols), f32)],
         scratch_shapes=scratch,
-        compiler_params=pltpu.CompilerParams(collective_id=0, has_side_effects=True, vmem_limit_bytes=60 << 20),
+        compiler_params=pltpu.CompilerParams(collective_id=0, has_side_effects=True, vmem_limit_bytes=52953088),
         name="correction",
     )(iterate[0, 0], forcing[0, 0], forward_state[0, 0], conductivity[0], terminal[0], *consts)
     return rn[None, None], gr[None]

time: 174 us -> 171 us (0.983)
  local copies, waits for them, and re-layouts: 3.85 us -> 1.98 us
    unnamed x4 -> x2, local copies, waits for them, and re-layouts: 3.85 us -> 1.98 us
where the time goes in v3:
time: 171 us
  Pallas kernels  169 us (99%)
  local copies, waits for them, and re-layouts  1.98 us (1%)
    pallas_call x1, Pallas kernels, body(): pl.pallas_call(functools.partial(kernel, rows, cols, steps, layers), in_s...  169 us

profile of v3, /device:TPU:1, one launch (start us, length us, event | category | flops | bytes accessed | tf_op | source)
XLA Modules:
  0.0 171.2 jit_solution(16224772029210510675)
XLA Ops:
  0.6 168.6 %correction.1 = (f32[512,1024]{1,0:T(8,128)S(1)}, f32[32,1024]{1,0:T(8,128)S(1)}) custom-call(f32[512,1024]{1,0:T(8,128)} %bitcast.9, f32[512,1024]{1,0:T(8,128)} %bitcast.10, f32[512,1024]{1,0:T(8,128)} %bitcast.11, f32[512,1024]{1,0:T(8,128)} %bitcast.12, f32[512,1024]{1,0:T(8,128)} %bitcast.13, bf16[6,1024,1024]{2,1,0:T(8,128)(2,1)} %constant.4.clone.tab_h, ...), custom_call_target="tpu_custom_call" | custom-call | tf_op jit(solution)/shard_map/correction/pallas_call | solution.py:567
  169.2 1.3 copy.11
  170.5 0.7 copy.12

commit v4 on v3

--- a/solution.py
+++ b/solution.py
@@ -15,7 +15,7 @@
 MESH = pl.DeviceIdType.MESH
 stride = 37
 parts = 4
-FS1, FS2 = 32,96
+FS1, FS2 = 24, 90
 f32, bf16 = jnp.float32, jnp.bfloat16
 
 

time: 171 us -> 171 us (level)
  no operation moved by 1% of the time
where the time goes in v4:
time: 171 us
  Pallas kernels  168 us (98%)
  local copies, waits for them, and re-layouts  1.98 us (1%)
    pallas_call x1, Pallas kernels, body(): pl.pallas_call(functools.partial(kernel, rows, cols, steps, layers), in_s...  168 us

profile of v4, /device:TPU:1, one launch (start us, length us, event | category | flops | bytes accessed | tf_op | source)
XLA Modules:
  0.0 170.9 jit_solution(17378093877021534252)
XLA Ops:
  0.6 168.2 %correction.1 = (f32[512,1024]{1,0:T(8,128)S(1)}, f32[32,1024]{1,0:T(8,128)S(1)}) custom-call(f32[512,1024]{1,0:T(8,128)} %bitcast.9, f32[512,1024]{1,0:T(8,128)} %bitcast.10, f32[512,1024]{1,0:T(8,128)} %bitcast.11, f32[512,1024]{1,0:T(8,128)} %bitcast.12, f32[512,1024]{1,0:T(8,128)} %bitcast.13, bf16[6,1024,1024]{2,1,0:T(8,128)(2,1)} %constant.4.clone.tab_h, ...), custom_call_target="tpu_custom_call" | custom-call | tf_op jit(solution)/shard_map/correction/pallas_call | solution.py:567
  168.9 1.3 copy.11
  170.2 0.7 copy.12
